TPU v7x, 32 devices: a whole 2x2x4 slice. The times are simulated.
32 devices in a mesh: groups: 1, row: 16 (over z, y, core), col: 2 (over x), rep: 1.
Axes of the slice: x: 2, y: 2, z: 4, core: 2. Of those that a mesh axis runs over, the one named last changes fastest.
Arguments:
- bins: bfloat16 [256, 1536], P(('groups', 'row', 'col')), may hold values from -6 to 6
- row_proj: bfloat16 [96, 1536], P('rep'), may hold values from -0.15625 to 0.15625
- col_proj: bfloat16 [96, 1536], P('rep'), may hold values from -0.15625 to 0.15625
- conv_weight: bfloat16 [3, 9, 96, 96], P(None, None, 'rep'), may hold values from -0.21875 to 0.21875
- conv_bias: float32 [3, 96], P(None, 'rep'), may hold values from -3 to 3
Outputs:
- contact_map: bfloat16 [96, 256, 256], P('rep', ('groups', 'row'), 'col')
All inputs are finite; a program needn't handle non-finite values.
Results may differ from a plain program's by a relative error of at most 0.013.
Values may be sent and summed in bfloat16 or wider, within the bound.
A program may use at most 128 MiB of HBM per device.

v0:
```python
import jax
import jax.numpy as jnp
from jax import lax
from jax.sharding import PartitionSpec as P


def with_halo(value, sides, width):
    for axis, dim in sides:
        devices, length = (lax.axis_size(axis), value.shape[dim])
        up = [(i, (i + 1) % devices) for i in range(devices - 1)]
        down = [(j, i) for i, j in up]
        last = lax.slice_in_dim(value, length - width, length, axis=dim)
        leading = lax.slice_in_dim(value, 0, width, axis=dim)
        before = lax.ppermute(last, axis, up)
        after = lax.ppermute(leading, axis, down)
        value = jnp.concatenate([before, value, after], axis=dim)
    return value


def conv_valid(padded, filters, spread, height, breadth):
    total = None
    for tap in range(9):
        first = tap // 3 * spread
        second = tap % 3 * spread
        window = padded[:, first : first + height, second : second + breadth]
        term = jnp.einsum("oi,ipq->opq", filters[tap], window, preferred_element_type=jnp.float32)
        total = term if total is None else total + term
    return total


def layer_step(state, filters, bias_row, spread):
    active = jnp.maximum(state, 0)
    whole = lax.all_gather(active, "rep", axis=0, tiled=True)
    padded = with_halo(whole, (("row", 1), ("col", 2)), spread)
    height = state.shape[1]
    breadth = state.shape[2]
    conv = conv_valid(padded, filters, spread, height, breadth)
    return (state.astype(jnp.float32) + conv + bias_row[:, None, None]).astype(jnp.bfloat16)


def outer_terms(left_terms, right_terms):
    return (
        left_terms.T.astype(jnp.float32)[:, :, None] * right_terms.T.astype(jnp.float32)[:, None, :]
    ).astype(jnp.bfloat16)


def whole_terms(row_terms, col_terms):
    return (
        lax.all_gather(row_terms, "rep", axis=1, tiled=True),
        lax.all_gather(col_terms, "rep", axis=1, tiled=True),
    )


def whole_filters(conv_weight, conv_bias):
    return (
        lax.all_gather(
            conv_weight.astype(jnp.float32).astype(jnp.bfloat16), "rep", axis=2, tiled=True
        ).astype(jnp.float32),
        lax.all_gather(conv_bias.astype(jnp.bfloat16), "rep", axis=1, tiled=True).astype(
            conv_bias.dtype
        ),
    )


def project_bins(bins, weights):
    return lax.dot_general(
        bins, weights, (((1,), (1,)), ((), ())), preferred_element_type=jnp.float32
    ).astype(jnp.bfloat16)


def shards(bins, row_proj, col_proj, conv_weight, conv_bias):
    span = bins.shape[0]
    rows_count = lax.axis_size("row")
    cols_count = lax.axis_size("col")
    total_bins = span * rows_count * cols_count
    tile_rows = total_bins // rows_count
    tile_cols = total_bins // cols_count
    row_index = lax.axis_index("row")
    col_index = lax.axis_index("col")
    row_local = project_bins(bins, row_proj)
    col_local = project_bins(bins, col_proj)
    row_terms, col_terms = (
        lax.all_gather(row_local, ("row", "col"), axis=0, tiled=True),
        lax.all_gather(col_local, ("row", "col"), axis=0, tiled=True),
    )
    all_rows = None
    all_cols = None
    all_filters = None
    all_bias = None
    own_rows = lax.dynamic_slice_in_dim(row_terms, row_index * tile_rows, tile_rows, 0)
    own_cols = lax.dynamic_slice_in_dim(col_terms, col_index * tile_cols, tile_cols, 0)
    state = outer_terms(own_rows, own_cols)
    state = layer_step(state, conv_weight[0], conv_bias[0], 1)
    state = layer_step(state, conv_weight[1], conv_bias[1], 2)
    half = state.shape[0]
    all_rows, all_cols = whole_terms(row_terms, col_terms)
    wide_filters, all_bias = whole_filters(conv_weight, conv_bias)
    all_filters = wide_filters.astype(jnp.bfloat16)
    first_filters = all_filters[0]
    first_bias = all_bias[0]
    margin = 3
    padded_rows = jnp.pad(all_rows, ((margin, margin), (0, 0)))
    padded_cols = jnp.pad(all_cols, ((margin, margin), (0, 0)))
    mirror_rows = lax.dynamic_slice_in_dim(
        padded_rows, col_index * tile_cols, tile_cols + 2 * margin, 0
    )
    mirror_cols = lax.dynamic_slice_in_dim(
        padded_cols, row_index * tile_rows, tile_rows + 2 * margin, 0
    )
    seed_map = outer_terms(mirror_rows, mirror_cols)
    inner_height = tile_cols + 4
    inner_breadth = tile_rows + 4
    conv_first = conv_valid(jnp.maximum(seed_map, 0), first_filters, 1, inner_height, inner_breadth)
    first_map = seed_map[:, 1:-1, 1:-1].astype(jnp.float32) + conv_first + first_bias[:, None, None]
    row_place = col_index * tile_cols - 2 + lax.iota(jnp.int32, inner_height)
    col_place = row_index * tile_rows - 2 + lax.iota(jnp.int32, inner_breadth)
    row_inside = (row_place >= 0) & (row_place < total_bins)
    col_inside = (col_place >= 0) & (col_place < total_bins)
    inside = row_inside[:, None] & col_inside[None, :]
    first_map = jnp.where(inside[None], first_map, 0.0).astype(jnp.bfloat16)
    own_half = lax.dynamic_slice_in_dim(first_map, lax.axis_index("rep") * half, half, 0)
    conv_second = conv_valid(jnp.maximum(first_map, 0), conv_weight[1], 2, tile_cols, tile_rows)
    second_map = (
        own_half[:, 2:-2, 2:-2].astype(jnp.float32) + conv_second + conv_bias[1][:, None, None]
    ).astype(jnp.bfloat16)
    mirror = second_map.transpose(0, 2, 1)
    state = ((state.astype(jnp.float32) + mirror.astype(jnp.float32)) * 0.5).astype(jnp.bfloat16)
    state = layer_step(state, conv_weight[2], conv_bias[2], 4)
    return state


def solution(mesh):
    placed = (
        P(("groups", "row", "col"), None),
        P("rep", None),
        P("rep", None),
        P(None, None, "rep", None),
        P(None, "rep"),
    )
    return jax.shard_map(
        shards,
        mesh=mesh,
        in_specs=placed,
        out_specs=P("rep", ("groups", "row"), "col"),
        check_vma=False,
    )
```

profile of v0, /device:TPU:0, one launch (start us, length us, event | category | flops | bytes accessed | tf_op | source)
XLA Modules:
  0.0 192.9 jit_solution(17881068901938080513)
XLA Ops:
  0.0 1.0 copy-done
  1.0 0.9 convolution_convert_fusion
  1.9 70.0 %all_gather.5 = bf16[256,96]{1,0:T(8,128)(2,1)S(1)} all-gather(bf16[8,96]{1,0:T(8,128)(2,1)S(1)} %convolution_convert_fusion), channel_id=1, replica_groups=mesh['groups'=1,'row'=16,'col'=2,'rep'=1] {'row','col'}, dimensions={0}, use_global_device_ids=true | all-gather | bytes 50688 | tf_op jit(solution)/shard_map/all_gather | solution.py:84
  71.9 1.1 convolution_convert_fusion.1
  73.0 63.7 %all_gather.4 = bf16[256,96]{1,0:T(8,128)(2,1)S(1)} all-gather(bf16[8,96]{1,0:T(8,128)(2,1)S(1)} %convolution_convert_fusion.1), channel_id=1, replica_groups=mesh['groups'=1,'row'=16,'col'=2,'rep'=1] {'row','col'}, dimensions={0}, use_global_device_ids=true | all-gather | bytes 50688 | tf_op jit(solution)/shard_map/all_gather | solution.py:83
  136.9 1.4 collective-permute-start
  138.3 1.3 collective-permute-start.1
  140.0 0.3 fusion.49
  140.3 0.3 convolution_add_fusion.7
  140.7 0.3 convolution_add_fusion.6
  141.0 0.4 convolution_add_fusion.5
  141.4 0.4 convolution_add_fusion.4
  141.8 0.4 convolution_add_fusion.3
  142.1 0.4 convolution_add_fusion.2
  142.5 0.4 convolution_add_fusion.1
  143.0 0.9 broadcast_maximum_fusion.1
  144.7 0.3 convolution_add_fusion.20
  145.1 0.3 convolution_add_fusion.19
  145.4 0.3 convolution_add_fusion.18
  145.7 0.3 convolution_add_fusion.17
  146.0 0.3 convolution_add_fusion.16
  146.3 0.4 fusion.39
  147.1 4.2 %collective-permute-start.2 = (bf16[96,18,1]{0,2,1:T(2,128)(2,1)S(1)}, bf16[96,18,1]{0,2,1:T(2,128)(2,1)S(1)}, u32[]{:S(2)}, u32[]{:S(2)}) collective-permute-start(bf16[96,18,1]{0,2,1:T(2,128)(2,1)S(1)} %get-tuple-element.15), channel_id=1, source_target_pairs={{0,1},{2,3},{4,5},{6,7},{8,9},{10,11},{12,13},{14,15},{16,17},{18,... | collective-permute-start | bytes 10376 | tf_op jit(solution)/shard_map/ppermute | solution.py:14
  151.3 1.3 collective-permute-start.3
  152.6 0.3 fusion.66
  153.2 3.6 %collective-permute-done.3 = bf16[96,18,1]{0,2,1:T(2,128)(2,1)S(1)} collective-permute-done((bf16[96,18,1]{0,2,1:T(2,128)(2,1)S(1)}, bf16[96,18,1]{0,2,1:T(2,128)(2,1)S(1)}, u32[]{:S(2)}, u32[]{:S(2)}) %collective-permute-start.3) | collective-permute-done | bytes 3488 | tf_op jit(solution)/shard_map/ppermute | solution.py:15
  158.3 0.4 fusion.28
  158.8 0.6 broadcast_maximum_fusion.3
  159.4 1.6 collective-permute-start.4
  161.0 1.3 collective-permute-start.5
  162.7 1.5 collective-permute-done.5
  164.2 1.9 %collective-permute-start.6 = (bf16[96,20,2]{0,2,1:T(2,128)(2,1)S(1)}, bf16[96,20,2]{0,2,1:T(2,128)(2,1)S(1)}, u32[]{:S(2)}, u32[]{:S(2)}) collective-permute-start(bf16[96,20,2]{0,2,1:T(2,128)(2,1)S(1)} %get-tuple-element.11), channel_id=1, source_target_pairs={{0,1},{2,3},{4,5},{6,7},{8,9},{10,11},{12,13},{14,15},{16,17},{18,... | collective-permute-start | bytes 23048 | tf_op jit(solution)/shard_map/ppermute | solution.py:14
  166.2 1.5 collective-permute-start.7
  168.3 3.5 %collective-permute-done.7 = bf16[96,20,2]{0,2,1:T(2,128)(2,1)S(1)} collective-permute-done((bf16[96,20,2]{0,2,1:T(2,128)(2,1)S(1)}, bf16[96,20,2]{0,2,1:T(2,128)(2,1)S(1)}, u32[]{:S(2)}, u32[]{:S(2)}) %collective-permute-start.7) | collective-permute-done | bytes 7712 | tf_op jit(solution)/shard_map/ppermute | solution.py:15
  173.2 0.5 fusion.19
  173.7 0.6 broadcast_maximum_fusion.2
  174.4 2.9 %collective-permute-start.8 = (bf16[96,4,128]{0,2,1:T(8,128)(2,1)S(1)}, bf16[96,4,128]{0,2,1:T(8,128)(2,1)S(1)}, u32[]{:S(2)}, u32[]{:S(2)}) collective-permute-start(bf16[96,4,128]{0,2,1:T(8,128)(2,1)S(1)} %get-tuple-element.17), channel_id=1, source_target_pairs={{0,2},{2,4},{4,6},{6,8},{8,10},{10,12},{12,14},{14,16},{16,18},{18... | collective-permute-start | bytes 294920 | tf_op jit(solution)/shard_map/ppermute | solution.py:14
  177.3 1.3 collective-permute-start.9
  178.6 2.8 %collective-permute-done.9 = bf16[96,4,128]{0,2,1:T(8,128)(2,1)S(1)} collective-permute-done((bf16[96,4,128]{0,2,1:T(8,128)(2,1)S(1)}, bf16[96,4,128]{0,2,1:T(8,128)(2,1)S(1)}, u32[]{:S(2)}, u32[]{:S(2)}) %collective-permute-start.9) | collective-permute-done | bytes 98336 | tf_op jit(solution)/shard_map/ppermute | solution.py:15
  181.5 1.6 collective-permute-start.10
  183.2 1.3 collective-permute-start.11
  184.8 4.1 %collective-permute-done.11 = bf16[96,24,4]{0,1,2:T(8,128)(2,1)S(1)} collective-permute-done((bf16[96,24,4]{0,1,2:T(8,128)(2,1)S(1)}, bf16[96,24,4]{0,1,2:T(8,128)(2,1)S(1)}, u32[]{:S(2)}, u32[]{:S(2)}) %collective-permute-start.11) | collective-permute-done | bytes 18464 | tf_op jit(solution)/shard_map/ppermute | solution.py:15
  188.9 0.3 maximum_maximum_fusion
  189.9 0.3 convolution_add_fusion.13
  190.5 0.3 convolution_add_fusion.11
  190.8 0.3 convolution_add_fusion.10
  191.4 0.4 fusion.36
  191.9 1.1 copy.128
  (58 shorter events, 7.7 us)
Async XLA Ops:
  0.0 1.0 copy-start
  136.7 3.3 %copy-start.2 = (f32[3,96]{1,0:T(4,128)S(1)}, f32[3,96]{1,0:T(4,128)}, u32[]{:S(2)}) copy-start(f32[3,96]{1,0:T(4,128)} %param.9) | copy-start | bytes 3460
  136.7 3.3 %copy-start.1 = (bf16[3,9,96,96]{3,2,1,0:T(8,128)(2,1)S(1)}, bf16[3,9,96,96]{3,2,1,0:T(8,128)(2,1)}, u32[]{:S(2)}) copy-start(bf16[3,9,96,96]{3,2,1,0:T(8,128)(2,1)} %param.8) | copy-start | bytes 1492996
  136.9 10.2 %collective-permute-start = (bf16[96,1,128]{0,2,1:T(8,128)(2,1)S(1)}, bf16[96,1,128]{0,2,1:T(8,128)(2,1)S(1)}, u32[]{:S(2)}, u32[]{:S(2)}) collective-permute-start(bf16[96,1,128]{0,2,1:T(8,128)(2,1)S(1)} %get-tuple-element.21), channel_id=1, source_target_pairs={{0,2},{2,4},{4,6},{6,8},{8,10},{10,12},{12,14},{14,16},{16,18},{18... | collective-permute-start | bytes 73736 | tf_op jit(solution)/shard_map/ppermute | solution.py:14
  138.3 8.7 %collective-permute-start.1 = (bf16[96,1,128]{0,2,1:T(8,128)(2,1)S(1)}, bf16[96,1,128]{0,2,1:T(8,128)(2,1)S(1)}, u32[]{:S(2)}, u32[]{:S(2)}) collective-permute-start(bf16[96,1,128]{0,2,1:T(8,128)(2,1)S(1)} %get-tuple-element.22), channel_id=1, source_target_pairs={{2,0},{4,2},{6,4},{8,6},{10,8},{12,10},{14,12},{16,14},{18,16},{20... | collective-permute-start | bytes 73736 | tf_op jit(solution)/shard_map/ppermute | solution.py:15
  147.1 6.1 %collective-permute-start.2 = (bf16[96,18,1]{0,2,1:T(2,128)(2,1)S(1)}, bf16[96,18,1]{0,2,1:T(2,128)(2,1)S(1)}, u32[]{:S(2)}, u32[]{:S(2)}) collective-permute-start(bf16[96,18,1]{0,2,1:T(2,128)(2,1)S(1)} %get-tuple-element.15), channel_id=1, source_target_pairs={{0,1},{2,3},{4,5},{6,7},{8,9},{10,11},{12,13},{14,15},{16,17},{18,... | collective-permute-start | bytes 10376 | tf_op jit(solution)/shard_map/ppermute | solution.py:14
  151.3 5.6 %collective-permute-start.3 = (bf16[96,18,1]{0,2,1:T(2,128)(2,1)S(1)}, bf16[96,18,1]{0,2,1:T(2,128)(2,1)S(1)}, u32[]{:S(2)}, u32[]{:S(2)}) collective-permute-start(bf16[96,18,1]{0,2,1:T(2,128)(2,1)S(1)} %get-tuple-element.16), channel_id=1, source_target_pairs={{1,0},{3,2},{5,4},{7,6},{9,8},{11,10},{13,12},{15,14},{17,16},{19,... | collective-permute-start | bytes 10376 | tf_op jit(solution)/shard_map/ppermute | solution.py:15
  159.4 3.2 %collective-permute-start.4 = (bf16[96,2,128]{0,2,1:T(8,128)(2,1)S(1)}, bf16[96,2,128]{0,2,1:T(8,128)(2,1)S(1)}, u32[]{:S(2)}, u32[]{:S(2)}) collective-permute-start(bf16[96,2,128]{0,2,1:T(8,128)(2,1)S(1)} %get-tuple-element.19), channel_id=1, source_target_pairs={{0,2},{2,4},{4,6},{6,8},{8,10},{10,12},{12,14},{14,16},{16,18},{18... | collective-permute-start | bytes 147464 | tf_op jit(solution)/shard_map/ppermute | solution.py:14
  161.0 3.1 %collective-permute-start.5 = (bf16[96,2,128]{0,2,1:T(8,128)(2,1)S(1)}, bf16[96,2,128]{0,2,1:T(8,128)(2,1)S(1)}, u32[]{:S(2)}, u32[]{:S(2)}) collective-permute-start(bf16[96,2,128]{0,2,1:T(8,128)(2,1)S(1)} %get-tuple-element.20), channel_id=1, source_target_pairs={{2,0},{4,2},{6,4},{8,6},{10,8},{12,10},{14,12},{16,14},{18,16},{20... | collective-permute-start | bytes 147464 | tf_op jit(solution)/shard_map/ppermute | solution.py:15
  164.2 4.1 %collective-permute-start.6 = (bf16[96,20,2]{0,2,1:T(2,128)(2,1)S(1)}, bf16[96,20,2]{0,2,1:T(2,128)(2,1)S(1)}, u32[]{:S(2)}, u32[]{:S(2)}) collective-permute-start(bf16[96,20,2]{0,2,1:T(2,128)(2,1)S(1)} %get-tuple-element.11), channel_id=1, source_target_pairs={{0,1},{2,3},{4,5},{6,7},{8,9},{10,11},{12,13},{14,15},{16,17},{18,... | collective-permute-start | bytes 23048 | tf_op jit(solution)/shard_map/ppermute | solution.py:14
  166.2 5.6 %collective-permute-start.7 = (bf16[96,20,2]{0,2,1:T(2,128)(2,1)S(1)}, bf16[96,20,2]{0,2,1:T(2,128)(2,1)S(1)}, u32[]{:S(2)}, u32[]{:S(2)}) collective-permute-start(bf16[96,20,2]{0,2,1:T(2,128)(2,1)S(1)} %get-tuple-element.12), channel_id=1, source_target_pairs={{1,0},{3,2},{5,4},{7,6},{9,8},{11,10},{13,12},{15,14},{17,16},{19,... | collective-permute-start | bytes 23048 | tf_op jit(solution)/shard_map/ppermute | solution.py:15
  174.4 4.2 %collective-permute-start.8 = (bf16[96,4,128]{0,2,1:T(8,128)(2,1)S(1)}, bf16[96,4,128]{0,2,1:T(8,128)(2,1)S(1)}, u32[]{:S(2)}, u32[]{:S(2)}) collective-permute-start(bf16[96,4,128]{0,2,1:T(8,128)(2,1)S(1)} %get-tuple-element.17), channel_id=1, source_target_pairs={{0,2},{2,4},{4,6},{6,8},{8,10},{10,12},{12,14},{14,16},{16,18},{18... | collective-permute-start | bytes 294920 | tf_op jit(solution)/shard_map/ppermute | solution.py:14
  177.3 4.1 %collective-permute-start.9 = (bf16[96,4,128]{0,2,1:T(8,128)(2,1)S(1)}, bf16[96,4,128]{0,2,1:T(8,128)(2,1)S(1)}, u32[]{:S(2)}, u32[]{:S(2)}) collective-permute-start(bf16[96,4,128]{0,2,1:T(8,128)(2,1)S(1)} %get-tuple-element.18), channel_id=1, source_target_pairs={{2,0},{4,2},{6,4},{8,6},{10,8},{12,10},{14,12},{16,14},{18,16},{20... | collective-permute-start | bytes 294920 | tf_op jit(solution)/shard_map/ppermute | solution.py:15
  181.5 3.3 %collective-permute-start.10 = (bf16[96,24,4]{0,1,2:T(8,128)(2,1)S(1)}, bf16[96,24,4]{0,1,2:T(8,128)(2,1)S(1)}, u32[]{:S(2)}, u32[]{:S(2)}) collective-permute-start(bf16[96,24,4]{0,1,2:T(8,128)(2,1)S(1)} %copy.106), channel_id=1, source_target_pairs={{0,1},{2,3},{4,5},{6,7},{8,9},{10,11},{12,13},{14,15},{16,17},{18,... | collective-permute-start | bytes 55304 | tf_op jit(solution)/shard_map/ppermute | solution.py:14
  183.2 5.7 %collective-permute-start.11 = (bf16[96,24,4]{0,1,2:T(8,128)(2,1)S(1)}, bf16[96,24,4]{0,1,2:T(8,128)(2,1)S(1)}, u32[]{:S(2)}, u32[]{:S(2)}) collective-permute-start(bf16[96,24,4]{0,1,2:T(8,128)(2,1)S(1)} %copy.112), channel_id=1, source_target_pairs={{1,0},{3,2},{5,4},{7,6},{9,8},{11,10},{13,12},{15,14},{17,16},{19,... | collective-permute-start | bytes 55304 | tf_op jit(solution)/shard_map/ppermute | solution.py:15
where the time goes:
time: 195 us; the launch traced here: 193 us
  blocking collectives  134 us (69%)
  starting transfers between devices  21.7 us (11%)
  matrix products  17.8 us (9%)
  waiting for transfers between devices  15.5 us (8%)
  local copies, waits for them, and re-layouts  2.12 us (1%)
    all_gather x1, blocking collectives, shards(): lax.all_gather(col_local, ('row', 'col'), axis=0, tiled=True)  70 us
    all_gather x1, blocking collectives, shards(): lax.all_gather(row_local, ('row', 'col'), axis=0, tiled=True)  63.7 us
    dot_general x45, matrix products, conv_valid(): jnp.einsum('oi,ipq->opq', filters[tap], window, preferred_element_type=jn...  15.7 us
    ppermute x6, waiting for transfers between devices, with_halo(): after = lax.ppermute(leading, axis, down)  15.5 us
    ppermute x6, starting transfers between devices, with_halo(): before = lax.ppermute(last, axis, up)  13.7 us
    ppermute x6, starting transfers between devices, with_halo(): after = lax.ppermute(leading, axis, down)  7.93 us
  transfers between devices with their start and end apart: 12, of which 5 were waited for; matrix products, arithmetic and copies ran while one was open for 5% of the time, Pallas kernels for 0%

commit v1 on v0

v1 whole, which is shorter than its diff:
```python
import functools

import jax
import jax.numpy as jnp
from jax import lax
from jax.experimental import pallas as pl
from jax.experimental.pallas import tpu as pltpu
from jax.sharding import PartitionSpec as P

MESH = pl.DeviceIdType.MESH
EDGE = 8
LANES = 128
GROUP = 3 * LANES
WIDE = 4 * LANES
NT = (((1,), (1,)), ((), ()))


def gather_kernel(rows, cols, bins_ref, rp_ref, cp_ref, near_ref, far_ref, held, send_sem, recv_sem):
    count = rows * cols
    row_index = lax.axis_index("row")
    col_index = lax.axis_index("col")
    me = row_index * cols + col_index
    span, channels = bins_ref.shape[0], rp_ref.shape[0]

    def place(step):
        other = lax.rem(me + step, count)
        return {"row": lax.div(other, cols), "col": lax.rem(other, cols)}

    barrier = pltpu.get_barrier_semaphore()

    def greet(step, carry):
        pl.semaphore_signal(barrier, inc=1, device_id=place(step), device_id_type=MESH)
        return carry

    lax.fori_loop(1, count, greet, 0)
    bins = bins_ref[...]
    terms = [
        lax.dot_general(bins, ref[...], NT, preferred_element_type=jnp.float32)
        for ref in (rp_ref, cp_ref)
    ]
    block = jnp.concatenate(terms, axis=0)
    fill = jnp.zeros((2 * span, LANES - channels), jnp.float32)
    held[me] = jnp.concatenate([block, fill], axis=1).astype(jnp.bfloat16)
    near_ref[...] = jnp.zeros_like(near_ref)
    far_ref[...] = jnp.zeros_like(far_ref)
    pl.semaphore_wait(barrier, count - 1)

    def copy(step):
        return pltpu.make_async_remote_copy(
            src_ref=held.at[me],
            dst_ref=held.at[me],
            send_sem=send_sem.at[step],
            recv_sem=recv_sem.at[step],
            device_id=place(step),
            device_id_type=MESH,
        )

    def send(step, carry):
        copy(step).start()
        return carry

    def finish(step, carry):
        copy(step).wait()
        return carry

    lax.fori_loop(1, count, send, 0)
    lax.fori_loop(1, count, finish, 0)

    def lay(out_ref, first, blocks, offset):
        def one(index, carry):
            block_index = first + index

            @pl.when((block_index >= 0) & (block_index < count))
            def _():
                values = held[block_index].astype(jnp.float32)
                at = pl.ds(pl.multiple_of(offset + index * span, 8), span)
                out_ref[0, at, :] = values[:span]
                out_ref[1, at, :] = values[span:]

            return carry

        lax.fori_loop(0, blocks, one, 0)

    tile_rows = near_ref.shape[1] - 2 * EDGE
    tile_cols = far_ref.shape[1] - 4 * EDGE
    lay(near_ref, (row_index * tile_rows - EDGE) // span, (tile_rows + 2 * EDGE) // span, 0)
    lay(far_ref, (col_index * tile_cols - EDGE) // span, (tile_cols + 2 * EDGE) // span, EDGE)


def rounded(value):
    return value.astype(jnp.bfloat16).astype(jnp.float32)


def fill_filters(packed, slot, w_ref, layer, swapped, starts):
    channels = w_ref.shape[2]
    packed[slot] = jnp.zeros(packed.shape[1:], packed.dtype)
    for slab in range(4):
        for parity in range(2):
            first = slab - parity
            if 0 <= first <= 2:
                for second in range(3):
                    tap = 3 * second + first if swapped else 3 * first + second
                    lane = starts[slab] + second * LANES
                    packed[slot, parity * LANES : parity * LANES + channels, lane : lane + channels] = w_ref[
                        layer, tap
                    ]


def conv_kernel(total, near_ref, far_ref, w_ref, b_ref, out_ref, state, stacked, packed, result):
    channels, tile_rows, tile_cols = out_ref.shape
    pitch = tile_cols + 2 * EDGE
    frame = tile_rows + 2 * EDGE
    row_index = lax.axis_index("row")
    col_index = lax.axis_index("col")
    packs = (0, GROUP, 2 * GROUP, 3 * GROUP)
    last_packs = (0, GROUP, GROUP + WIDE, GROUP + 2 * WIDE)
    for layer in range(2):
        for swapped in range(2):
            fill_filters(packed, 2 * layer + swapped, w_ref, layer, swapped, packs)
    fill_filters(packed, 4, w_ref, 2, 0, last_packs)
    ones = (
        lax.broadcasted_iota(jnp.int32, (LANES, LANES), 0)
        == lax.broadcasted_iota(jnp.int32, (LANES, LANES), 1)
    ).astype(jnp.float32).astype(jnp.bfloat16)
    for parity in range(2):
        lane = last_packs[1 + parity] + GROUP
        packed[4, parity * LANES : (parity + 1) * LANES, lane : lane + LANES] = ones

    fill = jnp.zeros((1, LANES - channels), jnp.float32)
    biases = [jnp.concatenate([b_ref[l : l + 1, :], fill], axis=1) for l in range(3)]
    place = lax.broadcasted_iota(jnp.int32, (pitch, LANES), 0)
    low = jnp.maximum(EDGE - col_index * tile_cols, 0)
    high = jnp.minimum(pitch, total - col_index * tile_cols + EDGE)

    def masked(value, row):
        where = row_index * tile_rows - EDGE + row
        top = jnp.where((where >= 0) & (where < total), high, 0)
        return jnp.where((place >= low) & (place < top), value, 0.0)

    def at_row(row):
        return pl.ds(pl.multiple_of(EDGE + row * pitch, 8), pitch)

    base, spread = 2, 1
    groups = (frame - 2 * base) // (2 * spread)
    for side in range(2):
        for second in range(3):
            begin = EDGE + (second - 1) * spread
            shifted = far_ref[1 - side, begin : begin + pitch, :]

            def build(index, carry, side=side, second=second, shifted=shifted):
                for parity in range(2):
                    row = base - spread + 2 * index + parity
                    value = near_ref[side, pl.ds(row, 1), :] * shifted
                    at = pl.ds(pl.multiple_of(index * pitch, 16), pitch)
                    stacked[side, parity, at, second * LANES : (second + 1) * LANES] = jnp.maximum(
                        value, 0.0
                    ).astype(jnp.bfloat16)
                return carry

            lax.fori_loop(0, groups + 1, build, 0)

    def window(side, index, chunk):
        here = pl.ds(pl.multiple_of(index * chunk, 16), chunk)
        after = pl.ds(pl.multiple_of((index + 1) * chunk, 16), chunk)
        return jnp.concatenate(
            [stacked[side, p, at, :GROUP] for at in (here, after) for p in range(2)], axis=1
        )

    def first_layer(index, carry):
        for side in range(2):
            acc = lax.dot_general(
                window(side, index, pitch),
                packed[side, :, : 4 * GROUP],
                NT,
                preferred_element_type=jnp.float32,
            )
            for parity in range(2):
                row = base + 2 * index + parity
                old = near_ref[side, pl.ds(row, 1), :] * far_ref[1 - side, EDGE : EDGE + pitch, :]
                value = rounded(old) + acc[:, parity * LANES : (parity + 1) * LANES] + biases[0]
                state[side, at_row(row), :] = masked(rounded(value), row)
        return carry

    lax.fori_loop(0, groups, first_layer, 0)

    base1, spread1 = 4, 2
    groups1 = (frame - 2 * base1) // (2 * spread1)
    chunk1 = spread1 * pitch

    def build_second(index, carry):
        for side in range(2):
            for parity in range(2):
                for e in range(spread1):
                    row = base1 - spread1 + (2 * index + parity) * spread1 + e
                    at = pl.ds(pl.multiple_of(index * chunk1 + e * pitch, 16), pitch)
                    for second in range(3):
                        begin = EDGE + row * pitch + (second - 1) * spread1
                        value = jnp.maximum(state[side, pl.ds(begin, pitch), :], 0.0)
                        stacked[side, parity, at, second * LANES : (second + 1) * LANES] = value.astype(
                            jnp.bfloat16
                        )
        return carry

    lax.fori_loop(0, groups1 + 1, build_second, 0)

    def second_layer(index, carry):
        accs = [
            lax.dot_general(
                window(side, index, chunk1),
                packed[2 + side, :, : 4 * GROUP],
                NT,
                preferred_element_type=jnp.float32,
            )
            for side in range(2)
        ]
        for parity in range(2):
            for e in range(spread1):
                row = base1 + (2 * index + parity) * spread1 + e
                both = [
                    rounded(
                        state[side, at_row(row), :]
                        + accs[side][e * pitch : (e + 1) * pitch, parity * LANES : (parity + 1) * LANES]
                        + biases[1]
                    )
                    for side in range(2)
                ]
                state[0, at_row(row), :] = masked(rounded((both[0] + both[1]) * 0.5), row)
        return carry

    lax.fori_loop(0, groups1, second_layer, 0)

    base2, spread2 = EDGE, 4
    groups2 = tile_rows // (2 * spread2)
    chunk2 = spread2 * tile_cols

    def build_third(index, carry):
        for parity in range(2):
            for e in range(spread2):
                row = base2 - spread2 + (2 * index + parity) * spread2 + e
                at = pl.ds(pl.multiple_of(index * chunk2 + e * tile_cols, 16), tile_cols)
                for second in range(3):
                    begin = 2 * EDGE + row * pitch + (second - 1) * spread2
                    value = state[0, pl.ds(begin, tile_cols), :]
                    if second == 1:
                        stacked[0, parity, at, GROUP:] = value.astype(jnp.bfloat16)
                    stacked[0, parity, at, second * LANES : (second + 1) * LANES] = jnp.maximum(
                        value, 0.0
                    ).astype(jnp.bfloat16)
        return carry

    lax.fori_loop(0, groups2 + 1, build_third, 0)
    bias_rows = jnp.broadcast_to(biases[2], (LANES, LANES)).T[:channels]
    bias_rows = jnp.concatenate([bias_rows] * (tile_cols // LANES), axis=1)

    def third_layer(index, carry):
        here = pl.ds(pl.multiple_of(index * chunk2, 16), chunk2)
        after = pl.ds(pl.multiple_of((index + 1) * chunk2, 16), chunk2)
        pieces = [
            stacked[0, 0, here, :GROUP],
            stacked[0, 1, here, :],
            stacked[0, 0, after, :],
            stacked[0, 1, after, :GROUP],
        ]
        acc = lax.dot_general(
            packed[4], jnp.concatenate(pieces, axis=1), NT, preferred_element_type=jnp.float32
        )
        for parity in range(2):
            for e in range(spread2):
                row = (2 * index + parity) * spread2 + e
                value = (
                    acc[parity * LANES : parity * LANES + channels, e * tile_cols : (e + 1) * tile_cols]
                    + bias_rows
                )
                result[pl.ds(row, channels, stride=tile_rows), :] = value
        return carry

    lax.fori_loop(0, groups2, third_layer, 0)
    out_ref[...] = result[...].reshape(channels, tile_rows, tile_cols).astype(jnp.bfloat16)


def shards(bins, row_proj, col_proj, conv_weight, conv_bias):
    rows = lax.axis_size("row")
    cols = lax.axis_size("col")
    reps = lax.axis_size("rep")
    own = conv_bias.shape[1]
    if reps > 1:
        row_proj = lax.all_gather(row_proj, "rep", axis=0, tiled=True)
        col_proj = lax.all_gather(col_proj, "rep", axis=0, tiled=True)
        conv_weight = lax.all_gather(conv_weight, "rep", axis=2, tiled=True)
        conv_bias = lax.all_gather(conv_bias, "rep", axis=1, tiled=True)
    span = bins.shape[0]
    count = rows * cols
    total = span * count
    tile_rows = total // rows
    tile_cols = total // cols
    channels = conv_bias.shape[1]
    frame = tile_rows + 2 * EDGE
    pitch = tile_cols + 2 * EDGE
    vmem = pl.BlockSpec(memory_space=pltpu.VMEM)
    near, far = pl.pallas_call(
        functools.partial(gather_kernel, rows, cols),
        out_shape=[
            jax.ShapeDtypeStruct((2, frame, LANES), jnp.float32),
            jax.ShapeDtypeStruct((2, pitch + 2 * EDGE, LANES), jnp.float32),
        ],
        in_specs=[vmem] * 3,
        out_specs=[vmem] * 2,
        scratch_shapes=[
            pltpu.VMEM((count, 2 * span, LANES), jnp.bfloat16),
            pltpu.SemaphoreType.DMA((count,)),
            pltpu.SemaphoreType.DMA((count,)),
        ],
        compiler_params=pltpu.CompilerParams(
            collective_id=0, has_side_effects=True, vmem_limit_bytes=16 * 2**20
        ),
        name="gather_terms",
    )(bins, row_proj, col_proj)
    out = pl.pallas_call(
        functools.partial(conv_kernel, total),
        out_shape=jax.ShapeDtypeStruct((channels, tile_rows, tile_cols), jnp.bfloat16),
        in_specs=[vmem] * 4,
        out_specs=vmem,
        scratch_shapes=[
            pltpu.VMEM((2, frame * pitch + 2 * EDGE, LANES), jnp.float32),
            pltpu.VMEM((2, 2, frame // 2 * pitch, WIDE), jnp.bfloat16),
            pltpu.VMEM((5, 2 * LANES, 2 * GROUP + 2 * WIDE), jnp.bfloat16),
            pltpu.VMEM((channels * tile_rows, tile_cols), jnp.float32),
        ],
        compiler_params=pltpu.CompilerParams(vmem_limit_bytes=58 * 2**20),
        name="conv_stack",
    )(near, far, conv_weight, conv_bias)
    if reps > 1:
        out = lax.dynamic_slice_in_dim(out, lax.axis_index("rep") * own, own, 0)
    return out


def solution(mesh):
    placed = (
        P(("groups", "row", "col"), None),
        P("rep", None),
        P("rep", None),
        P(None, None, "rep", None),
        P(None, "rep"),
    )
    return jax.shard_map(
        shards,
        mesh=mesh,
        in_specs=placed,
        out_specs=P("rep", ("groups", "row"), "col"),
        check_vma=False,
    )
```

time: 195 us -> 36.3 us (0.19)
  blocking collectives: 134 us -> 0 us
  Pallas kernels: 0 us -> 32.1 us
  starting transfers between devices: 21.7 us -> 0 us
  matrix products: 17.8 us -> 0 us
  waiting for transfers between devices: 15.5 us -> 0 us
    all_gather x2 -> x0, blocking collectives: 134 us -> none  [the longest x1 70 us: shards(): lax.all_gather(col_local, ('row', 'col'), axis=0, tiled=True)]
    pallas_call x0 -> x2, Pallas kernels: none -> 32.1 us  [the longest x1 21.2 us: shards(): pl.pallas_call(functools.partial(conv_kernel, total), out_shape=jax.Shape...]
    ppermute x12 -> x0, starting transfers between devices: 21.7 us -> none  [the longest x6 13.7 us: with_halo(): before = lax.ppermute(last, axis, up)]
    dot_general x47 -> x0, matrix products: 17.8 us -> none  [the longest x45 15.7 us: conv_valid(): jnp.einsum('oi,ipq->opq', filters[tap], window, preferred_element_type=jn...]
    ppermute x12 -> x0, waiting for transfers between devices: 15.5 us -> none  [the longest x6 15.5 us: with_halo(): after = lax.ppermute(leading, axis, down)]
    unnamed x6 -> x10, local copies, waits for them, and re-layouts: 0.97 us -> 3.91 us
  transfers between devices with their start and end apart: 12 -> 0, of which waited for: 5 -> 0; matrix products, arithmetic and copies ran while one was open for 5% -> 0% of each run, Pallas kernels for 0% -> 0%
where the time goes in v1:
time: 36.3 us; the launch traced here: 36.1 us
  Pallas kernels  32.1 us (88%)
  local copies, waits for them, and re-layouts  3.91 us (11%)
    pallas_call x1, Pallas kernels, shards(): pl.pallas_call(functools.partial(conv_kernel, total), out_shape=jax.Shape...  21.2 us
    pallas_call x1, Pallas kernels, shards(): pl.pallas_call(functools.partial(gather_kernel, rows, cols), out_shape=[j...  10.9 us
    unnamed x10, local copies, waits for them, and re-layouts  3.91 us

profile of v1, /device:TPU:0, one launch (start us, length us, event | category | flops | bytes accessed | tf_op | source)
XLA Modules:
  0.0 36.1 jit_solution(11672184772804499782)
XLA Ops:
  0.0 0.0 copy-start
  0.0 1.0 %copy-done = bf16[96,1536]{1,0:T(8,128)(2,1)S(1)} copy-done((bf16[96,1536]{1,0:T(8,128)(2,1)S(1)}, bf16[96,1536]{1,0:T(8,128)(2,1)}, u32[]{:S(2)}) %copy-start) | copy-done | bytes 294936
  1.0 0.0 copy-start.1
  1.0 1.0 %copy-done.1 = bf16[96,1536]{1,0:T(8,128)(2,1)S(1)} copy-done((bf16[96,1536]{1,0:T(8,128)(2,1)S(1)}, bf16[96,1536]{1,0:T(8,128)(2,1)}, u32[]{:S(2)}) %copy-start.1) | copy-done | bytes 294936
  1.9 0.0 copy-start.4
  1.9 0.7 %copy-done.4 = bf16[8,1536]{1,0:T(8,128)(2,1)S(1)} copy-done((bf16[8,1536]{1,0:T(8,128)(2,1)S(1)}, bf16[8,1536]{1,0:T(8,128)(2,1)}, u32[]{:S(2)}) %copy-start.4) | copy-done | bytes 24600
  2.7 10.9 %gather_terms.1 = (f32[2,32,128]{2,1,0:T(8,128)S(1)}, f32[2,160,128]{2,1,0:T(8,128)S(1)}) custom-call(bf16[8,1536]{1,0:T(8,128)(2,1)S(1)} %copy-done.4, bf16[96,1536]{1,0:T(8,128)(2,1)S(1)} %copy-done, bf16[96,1536]{1,0:T(8,128)(2,1)S(1)} %copy-done.1), custom_call_target="tpu_custom_call" | custom-call | tf_op jit(solution)/shard_map/gather_terms/pallas_call | solution.py:300
  13.6 0.0 copy-start.2
  13.6 0.7 %copy-done.2 = f32[2,160,128]{2,1,0:T(8,128)} copy-done((f32[2,160,128]{2,1,0:T(8,128)}, f32[2,160,128]{2,1,0:T(8,128)S(1)}, u32[]{:S(2)}) %copy-start.2) | copy-done | bytes 163864
  14.2 0.0 copy-start.3
  14.2 0.6 %copy-done.3 = f32[2,32,128]{2,1,0:T(8,128)} copy-done((f32[2,32,128]{2,1,0:T(8,128)}, f32[2,32,128]{2,1,0:T(8,128)S(1)}, u32[]{:S(2)}) %copy-start.3) | copy-done | bytes 32792
  14.8 21.2 %conv_stack.1 = bf16[96,16,128]{2,1,0:T(8,128)(2,1)} custom-call(f32[2,32,128]{2,1,0:T(8,128)} %copy-done.3, f32[2,160,128]{2,1,0:T(8,128)} %copy-done.2, bf16[3,9,96,96]{3,2,1,0:T(8,128)(2,1)} %w_ref.1, f32[3,96]{1,0:T(4,128)} %b_ref.1), custom_call_target="tpu_custom_call" | custom-call | tf_op jit(solution)/shard_map/conv_stack/pallas_call | solution.py:318
Async XLA Ops:
  0.0 1.0 %copy-start = (bf16[96,1536]{1,0:T(8,128)(2,1)S(1)}, bf16[96,1536]{1,0:T(8,128)(2,1)}, u32[]{:S(2)}) copy-start(bf16[96,1536]{1,0:T(8,128)(2,1)} %rp_ref.1) | copy-start | bytes 884740
  1.0 1.0 %copy-start.1 = (bf16[96,1536]{1,0:T(8,128)(2,1)S(1)}, bf16[96,1536]{1,0:T(8,128)(2,1)}, u32[]{:S(2)}) copy-start(bf16[96,1536]{1,0:T(8,128)(2,1)} %cp_ref.1) | copy-start | bytes 884740
  1.9 0.7 %copy-start.4 = (bf16[8,1536]{1,0:T(8,128)(2,1)S(1)}, bf16[8,1536]{1,0:T(8,128)(2,1)}, u32[]{:S(2)}) copy-start(bf16[8,1536]{1,0:T(8,128)(2,1)} %bins_ref.1) | copy-start | bytes 73732
  13.6 0.7 %copy-start.2 = (f32[2,160,128]{2,1,0:T(8,128)}, f32[2,160,128]{2,1,0:T(8,128)S(1)}, u32[]{:S(2)}) copy-start(f32[2,160,128]{2,1,0:T(8,128)S(1)} %get-tuple-element.8.far_ref) | copy-start | bytes 491524
  14.2 0.6 %copy-start.3 = (f32[2,32,128]{2,1,0:T(8,128)}, f32[2,32,128]{2,1,0:T(8,128)S(1)}, u32[]{:S(2)}) copy-start(f32[2,32,128]{2,1,0:T(8,128)S(1)} %get-tuple-element.7.near_ref) | copy-start | bytes 98308

commit v2 on v1

v2 whole, which is shorter than its diff:
```python
import functools

import jax
import jax.numpy as jnp
from jax import lax
from jax.experimental import pallas as pl
from jax.experimental.pallas import tpu as pltpu
from jax.sharding import PartitionSpec as P

MESH = pl.DeviceIdType.MESH
EDGE = 8
LANES = 128
GROUP = 3 * LANES
PAIR = 2 * GROUP
NT = (((1,), (1,)), ((), ()))
ROWS_PER_DOT = 1024


def rounded(value):
    return value.astype(jnp.bfloat16).astype(jnp.float32)


def share(groups, chunk):
    return max(n for n in range(1, groups + 1) if groups % n == 0 and (n == 1 or n * chunk <= ROWS_PER_DOT))


def decoder(
    rows,
    cols,
    bins_hbm,
    rp_hbm,
    cp_hbm,
    w_hbm,
    b_hbm,
    out_ref,
    bins_ref,
    rp_ref,
    cp_ref,
    w_ref,
    b_ref,
    held,
    near_ref,
    far_ref,
    state,
    stacked,
    packed,
    result,
    load_sem,
    send_sem,
    recv_sem,
):
    count = rows * cols
    row_index = lax.axis_index("row")
    col_index = lax.axis_index("col")
    me = row_index * cols + col_index
    span, channels = bins_ref.shape[0], rp_ref.shape[0]
    total = span * count
    _, tile_rows, tile_cols = out_ref.shape
    pitch = tile_cols + 2 * EDGE
    frame = tile_rows + 2 * EDGE

    loads = [
        pltpu.make_async_copy(source, target, load_sem.at[i])
        for i, (source, target) in enumerate(
            [(bins_hbm, bins_ref), (rp_hbm, rp_ref), (cp_hbm, cp_ref), (w_hbm, w_ref), (b_hbm, b_ref)]
        )
    ]
    for load in loads:
        load.start()

    def uses(block, other):
        near_block = lax.div(other, cols) * (tile_rows // span)
        far_block = lax.rem(other, cols) * (tile_cols // span)
        return ((block >= near_block - 1) & (block <= near_block + tile_rows // span)) | (
            (block >= far_block - 1) & (block <= far_block + tile_cols // span)
        )

    def ahead(step):
        return lax.rem(me + step, count)

    def behind(step):
        return lax.rem(me + count - step, count)

    def place(other):
        return {"row": lax.div(other, cols), "col": lax.rem(other, cols)}

    barrier = pltpu.get_barrier_semaphore()

    def greet(step, targets):
        @pl.when(uses(behind(step), me))
        def _():
            pl.semaphore_signal(barrier, inc=1, device_id=place(behind(step)), device_id_type=MESH)

        return targets + jnp.where(uses(me, ahead(step)), 1, 0)

    targets = lax.fori_loop(1, count, greet, 0)
    for load in loads[:3]:
        load.wait()
    bins = bins_ref[...]
    terms = [
        lax.dot_general(bins, ref[...], NT, preferred_element_type=jnp.float32)
        for ref in (rp_ref, cp_ref)
    ]
    blank = jnp.zeros((2 * span, LANES - channels), jnp.float32)
    held[me] = jnp.concatenate([jnp.concatenate(terms, axis=0), blank], axis=1).astype(jnp.bfloat16)
    pl.semaphore_wait(barrier, targets)

    def copy(step):
        return pltpu.make_async_remote_copy(
            src_ref=held.at[me],
            dst_ref=held.at[me],
            send_sem=send_sem.at[step],
            recv_sem=recv_sem.at[step],
            device_id=place(ahead(step)),
            device_id_type=MESH,
        )

    def send(step, carry):
        @pl.when(uses(me, ahead(step)))
        def _():
            copy(step).start()

        return carry

    lax.fori_loop(1, count, send, 0)

    near_ref[...] = jnp.zeros_like(near_ref)
    far_ref[...] = jnp.zeros_like(far_ref)
    packed[...] = jnp.zeros_like(packed)
    for load in loads[3:]:
        load.wait()
    for layer in range(3):
        for tap in range(9):
            filters = w_ref[layer, tap].astype(jnp.float32).T.astype(jnp.bfloat16)
            for swapped in range(2 if layer < 2 else 1):
                first, second = (tap % 3, tap // 3) if swapped else (tap // 3, tap % 3)
                for parity in range(2):
                    at = (first + parity) * GROUP + second * LANES
                    packed[
                        2 * layer + swapped,
                        at : at + channels,
                        parity * LANES : parity * LANES + channels,
                    ] = filters
    fill = jnp.zeros((1, LANES - channels), jnp.float32)
    biases = [jnp.concatenate([b_ref[l : l + 1, :], fill], axis=1) for l in range(3)]

    def finish(step, carry):
        @pl.when(uses(behind(step), me))
        def _():
            copy(step).wait_recv()

        return carry

    lax.fori_loop(1, count, finish, 0)

    def lay(out, first, blocks, offset):
        def one(index, carry):
            block = first + index

            @pl.when((block >= 0) & (block < count))
            def _():
                values = held[block].astype(jnp.float32)
                at = pl.ds(pl.multiple_of(offset + index * span, 8), span)
                out[0, at, :] = values[:span]
                out[1, at, :] = values[span:]

            return carry

        lax.fori_loop(0, blocks, one, 0)

    lay(near_ref, row_index * (tile_rows // span) - 1, frame // span, 0)
    lay(far_ref, col_index * (tile_cols // span) - 1, pitch // span, EDGE)

    position = lax.broadcasted_iota(jnp.int32, (pitch, LANES), 0)
    low = jnp.maximum(EDGE - col_index * tile_cols, 0)
    high = jnp.minimum(pitch, total - col_index * tile_cols + EDGE)

    def masked(value, row):
        where = row_index * tile_rows - EDGE + row
        top = jnp.where((where >= 0) & (where < total), high, 0)
        return jnp.where((position >= low) & (position < top), value, 0.0)

    def at_row(row):
        return pl.ds(pl.multiple_of(EDGE + row * pitch, 8), pitch)

    def convolved(side, slot, index, n, chunk):
        here = pl.ds(pl.multiple_of(index * (n * chunk), 16), n * chunk)
        after = pl.ds(pl.multiple_of(index * (n * chunk) + chunk, 16), n * chunk)
        return jnp.dot(
            jnp.concatenate([stacked[side, here, :], stacked[side, after, :]], axis=1),
            packed[slot],
            preferred_element_type=jnp.float32,
        )

    def outputs(n, chunk, spread):
        width = chunk // spread
        for group in range(n):
            for parity in range(2):
                for e in range(spread):
                    begin = group * chunk + e * width
                    yield (
                        (2 * group + parity) * spread + e,
                        slice(begin, begin + width),
                        slice(parity * LANES, (parity + 1) * LANES),
                    )

    base = 2
    groups = (frame - 2 * base) // 2
    for side in range(2):
        for second in range(3):
            begin = EDGE + second - 1
            shifted = far_ref[1 - side, begin : begin + pitch, :]

            def build(index, carry, side=side, second=second, shifted=shifted):
                for parity in range(2):
                    value = near_ref[side, pl.ds(base - 1 + 2 * index + parity, 1), :] * shifted
                    at = pl.ds(pl.multiple_of(index * pitch, 16), pitch)
                    lane = parity * GROUP + second * LANES
                    stacked[side, at, lane : lane + LANES] = jnp.maximum(value, 0.0).astype(jnp.bfloat16)
                return carry

            lax.fori_loop(0, groups + 1, build, 0)
    n0 = share(groups, pitch)

    def first_layer(index, carry):
        for side in range(2):
            acc = convolved(side, side, index, n0, pitch)
            for step, pixels, lanes in outputs(n0, pitch, 1):
                row = base + 2 * n0 * index + step
                old = near_ref[side, pl.ds(row, 1), :] * far_ref[1 - side, EDGE : EDGE + pitch, :]
                value = rounded(old) + acc[pixels, lanes] + biases[0]
                state[side, at_row(row), :] = masked(rounded(value), row)
        return carry

    lax.fori_loop(0, groups // n0, first_layer, 0)

    base1, spread1 = 4, 2
    groups1 = (frame - 2 * base1) // (2 * spread1)
    chunk1 = spread1 * pitch

    def build_second(index, carry):
        for side in range(2):
            for parity in range(2):
                for e in range(spread1):
                    row = base1 - spread1 + (2 * index + parity) * spread1 + e
                    at = pl.ds(pl.multiple_of(index * chunk1 + e * pitch, 16), pitch)
                    for second in range(3):
                        begin = EDGE + row * pitch + (second - 1) * spread1
                        value = jnp.maximum(state[side, pl.ds(begin, pitch), :], 0.0)
                        lane = parity * GROUP + second * LANES
                        stacked[side, at, lane : lane + LANES] = value.astype(jnp.bfloat16)
        return carry

    lax.fori_loop(0, groups1 + 1, build_second, 0)
    n1 = share(groups1, chunk1)

    def second_layer(index, carry):
        accs = [convolved(side, 2 + side, index, n1, chunk1) for side in range(2)]
        for step, pixels, lanes in outputs(n1, chunk1, spread1):
            row = base1 + 2 * n1 * spread1 * index + step
            both = [
                rounded(state[side, at_row(row), :] + accs[side][pixels, lanes] + biases[1])
                for side in range(2)
            ]
            state[0, at_row(row), :] = masked(rounded((both[0] + both[1]) * 0.5), row)
        return carry

    lax.fori_loop(0, groups1 // n1, second_layer, 0)

    base2, spread2 = EDGE, 4
    groups2 = tile_rows // (2 * spread2)
    chunk2 = spread2 * tile_cols

    def build_third(index, carry):
        for parity in range(2):
            for e in range(spread2):
                row = base2 - spread2 + (2 * index + parity) * spread2 + e
                at = pl.ds(pl.multiple_of(index * chunk2 + e * tile_cols, 16), tile_cols)
                for second in range(3):
                    begin = 2 * EDGE + row * pitch + (second - 1) * spread2
                    value = jnp.maximum(state[0, pl.ds(begin, tile_cols), :], 0.0)
                    lane = parity * GROUP + second * LANES
                    stacked[0, at, lane : lane + LANES] = value.astype(jnp.bfloat16)
        return carry

    lax.fori_loop(0, groups2 + 1, build_third, 0)
    n2 = share(groups2, chunk2)

    def third_layer(index, carry):
        acc = convolved(0, 4, index, n2, chunk2)
        for step, pixels, lanes in outputs(n2, chunk2, spread2):
            row = 2 * n2 * spread2 * index + step
            begin = pl.multiple_of(2 * EDGE + (base2 + row) * pitch, 8)
            value = state[0, pl.ds(begin, tile_cols), :] + acc[pixels, lanes] + biases[2]
            result[pl.ds(row, channels, stride=tile_rows), :] = value.T[:channels]
        return carry

    lax.fori_loop(0, groups2 // n2, third_layer, 0)
    out_ref[...] = result[...].reshape(channels, tile_rows, tile_cols).astype(jnp.bfloat16)

    def sent(step, carry):
        @pl.when(uses(me, ahead(step)))
        def _():
            copy(step).wait_send()

        return carry

    lax.fori_loop(1, count, sent, 0)


def shards(bins, row_proj, col_proj, conv_weight, conv_bias):
    rows = lax.axis_size("row")
    cols = lax.axis_size("col")
    reps = lax.axis_size("rep")
    own = conv_bias.shape[1]
    if reps > 1:
        row_proj = lax.all_gather(row_proj, "rep", axis=0, tiled=True)
        col_proj = lax.all_gather(col_proj, "rep", axis=0, tiled=True)
        conv_weight = lax.all_gather(conv_weight, "rep", axis=2, tiled=True)
        conv_bias = lax.all_gather(conv_bias, "rep", axis=1, tiled=True)
    span = bins.shape[0]
    count = rows * cols
    total = span * count
    tile_rows = total // rows
    tile_cols = total // cols
    channels = conv_bias.shape[1]
    frame = tile_rows + 2 * EDGE
    pitch = tile_cols + 2 * EDGE
    operands = (bins, row_proj, col_proj, conv_weight, conv_bias)
    out = pl.pallas_call(
        functools.partial(decoder, rows, cols),
        out_shape=jax.ShapeDtypeStruct((channels, tile_rows, tile_cols), jnp.bfloat16),
        in_specs=[pl.BlockSpec(memory_space=pltpu.MemorySpace.HBM)] * 5,
        out_specs=pl.BlockSpec(memory_space=pltpu.VMEM),
        scratch_shapes=[pltpu.VMEM(x.shape, x.dtype) for x in operands]
        + [
            pltpu.VMEM((count, 2 * span, LANES), jnp.bfloat16),
            pltpu.VMEM((2, frame, LANES), jnp.float32),
            pltpu.VMEM((2, pitch + 2 * EDGE, LANES), jnp.float32),
            pltpu.VMEM((2, frame * pitch + 2 * EDGE, LANES), jnp.float32),
            pltpu.VMEM((2, frame // 2 * pitch, PAIR), jnp.bfloat16),
            pltpu.VMEM((5, 2 * PAIR, 2 * LANES), jnp.bfloat16),
            pltpu.VMEM((channels * tile_rows, tile_cols), jnp.float32),
            pltpu.SemaphoreType.DMA((5,)),
            pltpu.SemaphoreType.DMA((count,)),
            pltpu.SemaphoreType.DMA((count,)),
        ],
        compiler_params=pltpu.CompilerParams(
            collective_id=0, has_side_effects=True, vmem_limit_bytes=60 * 2**20
        ),
        name="decode_map",
    )(*operands)
    if reps > 1:
        out = lax.dynamic_slice_in_dim(out, lax.axis_index("rep") * own, own, 0)
    return out


def solution(mesh):
    placed = (
        P(("groups", "row", "col"), None),
        P("rep", None),
        P("rep", None),
        P(None, None, "rep", None),
        P(None, "rep"),
    )
    return jax.shard_map(
        shards,
        mesh=mesh,
        in_specs=placed,
        out_specs=P("rep", ("groups", "row"), "col"),
        check_vma=False,
    )
```

time: 36.3 us -> 25.5 us (0.70)
  Pallas kernels: 32.1 us -> 23.6 us
  local copies, waits for them, and re-layouts: 3.91 us -> 1.77 us
    pallas_call x2 -> x1, Pallas kernels: 32.1 us -> 23.6 us  [shards(): pl.pallas_call(functools.partial(decoder, rows, cols), out_shape=jax.Shap...]
    unnamed x10 -> x1, local copies, waits for them, and re-layouts: 3.91 us -> 1.77 us
where the time goes in v2:
time: 25.5 us; the launch traced here: 25.4 us
  Pallas kernels  23.6 us (93%)
  local copies, waits for them, and re-layouts  1.77 us (7%)
    pallas_call x1, Pallas kernels, shards(): pl.pallas_call(functools.partial(decoder, rows, cols), out_shape=jax.Shap...  23.6 us
    unnamed x1, local copies, waits for them, and re-layouts  1.77 us

profile of v2, /device:TPU:0, one launch (start us, length us, event | category | flops | bytes accessed | tf_op | source)
XLA Modules:
  0.0 25.4 jit_solution(2635285615571359133)
XLA Ops:
  0.0 23.6 %decode_map.1 = bf16[96,16,128]{2,1,0:T(8,128)(2,1)} custom-call(bf16[8,1536]{1,0:T(8,128)(2,1)} %bins_hbm.1, bf16[96,1536]{1,0:T(8,128)(2,1)} %rp_hbm.1, bf16[96,1536]{1,0:T(8,128)(2,1)} %cp_hbm.1, bf16[3,9,96,96]{3,2,1,0:T(8,128)(2,1)} %w_hbm.1, f32[3,96]{1,0:T(4,128)} %b_hbm.1), custom_call_target="tpu_custom_call" | custom-call | tf_op jit(solution)/shard_map/decode_map/pallas_call | solution.py:330
  23.6 1.8 %copy.7 = bf16[96,16,128]{2,1,0:T(8,128)(2,1)} copy(bf16[96,16,128]{2,1,0:T(8,128)(2,1)} %decode_map.1) | data formatting | bytes 786432

commit v3 on v2

--- a/solution.py
+++ b/solution.py
@@ -13,7 +13,9 @@
 GROUP = 3 * LANES
 PAIR = 2 * GROUP
 NT = (((1,), (1,)), ((), ()))
-ROWS_PER_DOT = 1024
+ROWS_PER_DOT = 512
+MOST_CHUNKS = 16
+SPARE = 24 * 2**20
 
 
 def rounded(value):
@@ -58,6 +60,7 @@
     _, tile_rows, tile_cols = out_ref.shape
     pitch = tile_cols + 2 * EDGE
     frame = tile_rows + 2 * EDGE
+    apart = stacked.shape[0] - 2
 
     loads = [
         pltpu.make_async_copy(source, target, load_sem.at[i])
@@ -94,6 +97,9 @@
         return targets + jnp.where(uses(me, ahead(step)), 1, 0)
 
     targets = lax.fori_loop(1, count, greet, 0)
+    near_ref[...] = jnp.zeros_like(near_ref)
+    far_ref[...] = jnp.zeros_like(far_ref)
+    packed[...] = jnp.zeros_like(packed)
     for load in loads[:3]:
         load.wait()
     bins = bins_ref[...]
@@ -124,9 +130,6 @@
 
     lax.fori_loop(1, count, send, 0)
 
-    near_ref[...] = jnp.zeros_like(near_ref)
-    far_ref[...] = jnp.zeros_like(far_ref)
-    packed[...] = jnp.zeros_like(packed)
     for load in loads[3:]:
         load.wait()
     for layer in range(3):
@@ -171,21 +174,35 @@
     lay(near_ref, row_index * (tile_rows // span) - 1, frame // span, 0)
     lay(far_ref, col_index * (tile_cols // span) - 1, pitch // span, EDGE)
 
-    position = lax.broadcasted_iota(jnp.int32, (pitch, LANES), 0)
-    low = jnp.maximum(EDGE - col_index * tile_cols, 0)
-    high = jnp.minimum(pitch, total - col_index * tile_cols + EDGE)
+    cells = lax.broadcasted_iota(jnp.int32, (pitch, LANES), 0)
+    edge_cells = cells[:EDGE]
+    from_left = jnp.where(col_index > 0, 0, EDGE)
+    to_right = jnp.where(col_index < cols - 1, EDGE, 0)
+    from_top = jnp.where(row_index > 0, 0, pitch)
+    from_bottom = jnp.where(row_index < rows - 1, 0, pitch)
 
     def masked(value, row):
-        where = row_index * tile_rows - EDGE + row
-        top = jnp.where((where >= 0) & (where < total), high, 0)
-        return jnp.where((position >= low) & (position < top), value, 0.0)
+        left = jnp.where(edge_cells >= from_left, value[:EDGE], 0.0)
+        right = jnp.where(edge_cells < to_right, value[-EDGE:], 0.0)
+        value = jnp.concatenate([left, value[EDGE:-EDGE], right], axis=0)
+        if isinstance(row, int):
+            if row < EDGE:
+                value = jnp.where(cells >= from_top, value, 0.0)
+            elif row >= EDGE + tile_rows:
+                value = jnp.where(cells >= from_bottom, value, 0.0)
+            return value
+        start = jnp.where(row < EDGE, from_top, jnp.where(row >= EDGE + tile_rows, from_bottom, 0))
+        return jnp.where(cells >= start, value, 0.0)
+
+    def span_of(begin, size, unit=16):
+        return pl.ds(begin if isinstance(begin, int) else pl.multiple_of(begin, unit), size)
 
     def at_row(row):
-        return pl.ds(pl.multiple_of(EDGE + row * pitch, 8), pitch)
+        return span_of(EDGE + row * pitch, pitch, 8)
 
     def convolved(side, slot, index, n, chunk):
-        here = pl.ds(pl.multiple_of(index * (n * chunk), 16), n * chunk)
-        after = pl.ds(pl.multiple_of(index * (n * chunk) + chunk, 16), n * chunk)
+        here = span_of(index * (n * chunk), n * chunk)
+        after = span_of(index * (n * chunk) + chunk, n * chunk)
         return jnp.dot(
             jnp.concatenate([stacked[side, here, :], stacked[side, after, :]], axis=1),
             packed[slot],
@@ -204,98 +221,127 @@
                         slice(parity * LANES, (parity + 1) * LANES),
                     )
 
+    def pipeline(groups, n, build, multiply, store):
+        chunks = groups // n
+        if chunks > MOST_CHUNKS:
+            lax.fori_loop(0, groups + 1, lambda i, c: (build(i), c)[1], 0)
+            lax.fori_loop(0, chunks, lambda i, c: (store(i, multiply(i)), c)[1], 0)
+            return
+        for i in range(n + 1):
+            build(i)
+        held_acc = None
+        for i in range(chunks):
+            acc = multiply(i)
+            if i + 1 < chunks:
+                for j in range(n):
+                    build((i + 1) * n + 1 + j)
+            if held_acc is not None:
+                store(i - 1, held_acc)
+            held_acc = acc
+        store(chunks - 1, held_acc)
+
     base = 2
     groups = (frame - 2 * base) // 2
-    for side in range(2):
-        for second in range(3):
-            begin = EDGE + second - 1
-            shifted = far_ref[1 - side, begin : begin + pitch, :]
-
-            def build(index, carry, side=side, second=second, shifted=shifted):
-                for parity in range(2):
-                    value = near_ref[side, pl.ds(base - 1 + 2 * index + parity, 1), :] * shifted
-                    at = pl.ds(pl.multiple_of(index * pitch, 16), pitch)
+    n0 = share(groups, pitch)
+    halves = pitch // 16
+    shifted = [
+        [
+            far_ref[1 - side, EDGE + second - 1 : EDGE + second - 1 + pitch, :]
+            .astype(jnp.bfloat16)
+            .reshape(halves, 16, LANES)
+            for second in range(3)
+        ]
+        for side in range(2)
+    ]
+
+    def product(side, row, second):
+        line = jnp.broadcast_to(near_ref[side, pl.ds(row, 1), :], (16, LANES)).astype(jnp.bfloat16)
+        return (line[None] * shifted[side][second]).reshape(pitch, LANES)
+
+    def build_first(index):
+        for side in range(2):
+            for parity in range(2):
+                for second in range(3):
+                    value = product(side, base - 1 + 2 * index + parity, second)
                     lane = parity * GROUP + second * LANES
-                    stacked[side, at, lane : lane + LANES] = jnp.maximum(value, 0.0).astype(jnp.bfloat16)
-                return carry
-
-            lax.fori_loop(0, groups + 1, build, 0)
-    n0 = share(groups, pitch)
-
-    def first_layer(index, carry):
+                    stacked[side, span_of(index * pitch, pitch), lane : lane + LANES] = jnp.maximum(
+                        value, jnp.zeros_like(value)
+                    )
+
+    def store_first(index, accs):
         for side in range(2):
-            acc = convolved(side, side, index, n0, pitch)
             for step, pixels, lanes in outputs(n0, pitch, 1):
                 row = base + 2 * n0 * index + step
-                old = near_ref[side, pl.ds(row, 1), :] * far_ref[1 - side, EDGE : EDGE + pitch, :]
-                value = rounded(old) + acc[pixels, lanes] + biases[0]
+                old = product(side, row, 1).astype(jnp.float32)
+                value = old + accs[side][pixels, lanes] + biases[0]
                 state[side, at_row(row), :] = masked(rounded(value), row)
-        return carry
-
-    lax.fori_loop(0, groups // n0, first_layer, 0)
+
+    pipeline(
+        groups,
+        n0,
+        build_first,
+        lambda index: [convolved(side, side, index, n0, pitch) for side in range(2)],
+        store_first,
+    )
 
     base1, spread1 = 4, 2
     groups1 = (frame - 2 * base1) // (2 * spread1)
     chunk1 = spread1 * pitch
-
-    def build_second(index, carry):
+    n1 = share(groups1, chunk1)
+
+    def build_second(index):
         for side in range(2):
             for parity in range(2):
                 for e in range(spread1):
                     row = base1 - spread1 + (2 * index + parity) * spread1 + e
-                    at = pl.ds(pl.multiple_of(index * chunk1 + e * pitch, 16), pitch)
+                    at = span_of(index * chunk1 + e * pitch, pitch)
                     for second in range(3):
                         begin = EDGE + row * pitch + (second - 1) * spread1
                         value = jnp.maximum(state[side, pl.ds(begin, pitch), :], 0.0)
                         lane = parity * GROUP + second * LANES
-                        stacked[side, at, lane : lane + LANES] = value.astype(jnp.bfloat16)
-        return carry
-
-    lax.fori_loop(0, groups1 + 1, build_second, 0)
-    n1 = share(groups1, chunk1)
-
-    def second_layer(index, carry):
-        accs = [convolved(side, 2 + side, index, n1, chunk1) for side in range(2)]
+                        stacked[apart + side, at, lane : lane + LANES] = value.astype(jnp.bfloat16)
+
+    def store_second(index, accs):
         for step, pixels, lanes in outputs(n1, chunk1, spread1):
             row = base1 + 2 * n1 * spread1 * index + step
             both = [
                 rounded(state[side, at_row(row), :] + accs[side][pixels, lanes] + biases[1])
                 for side in range(2)
             ]
-            state[0, at_row(row), :] = masked(rounded((both[0] + both[1]) * 0.5), row)
-        return carry
-
-    lax.fori_loop(0, groups1 // n1, second_layer, 0)
+            state[2, at_row(row), :] = masked(rounded((both[0] + both[1]) * 0.5), row)
+
+    pipeline(
+        groups1,
+        n1,
+        build_second,
+        lambda index: [convolved(apart + side, 2 + side, index, n1, chunk1) for side in range(2)],
+        store_second,
+    )
 
     base2, spread2 = EDGE, 4
     groups2 = tile_rows // (2 * spread2)
     chunk2 = spread2 * tile_cols
-
-    def build_third(index, carry):
+    n2 = share(groups2, chunk2)
+
+    def build_third(index):
         for parity in range(2):
             for e in range(spread2):
                 row = base2 - spread2 + (2 * index + parity) * spread2 + e
-                at = pl.ds(pl.multiple_of(index * chunk2 + e * tile_cols, 16), tile_cols)
+                at = span_of(index * chunk2 + e * tile_cols, tile_cols)
                 for second in range(3):
                     begin = 2 * EDGE + row * pitch + (second - 1) * spread2
-                    value = jnp.maximum(state[0, pl.ds(begin, tile_cols), :], 0.0)
+                    value = jnp.maximum(state[2, pl.ds(begin, tile_cols), :], 0.0)
                     lane = parity * GROUP + second * LANES
                     stacked[0, at, lane : lane + LANES] = value.astype(jnp.bfloat16)
-        return carry
-
-    lax.fori_loop(0, groups2 + 1, build_third, 0)
-    n2 = share(groups2, chunk2)
-
-    def third_layer(index, carry):
-        acc = convolved(0, 4, index, n2, chunk2)
+
+    def store_third(index, acc):
         for step, pixels, lanes in outputs(n2, chunk2, spread2):
             row = 2 * n2 * spread2 * index + step
-            begin = pl.multiple_of(2 * EDGE + (base2 + row) * pitch, 8)
-            value = state[0, pl.ds(begin, tile_cols), :] + acc[pixels, lanes] + biases[2]
+            begin = span_of(2 * EDGE + (base2 + row) * pitch, tile_cols, 8)
+            value = state[2, begin, :] + acc[pixels, lanes] + biases[2]
             result[pl.ds(row, channels, stride=tile_rows), :] = value.T[:channels]
-        return carry
-
-    lax.fori_loop(0, groups2 // n2, third_layer, 0)
+
+    pipeline(groups2, n2, build_third, lambda index: convolved(0, 4, index, n2, chunk2), store_third)
     out_ref[...] = result[...].reshape(channels, tile_rows, tile_cols).astype(jnp.bfloat16)
 
     def sent(step, carry):
@@ -326,6 +372,7 @@
     channels = conv_bias.shape[1]
     frame = tile_rows + 2 * EDGE
     pitch = tile_cols + 2 * EDGE
+    stack = frame // 2 * pitch * PAIR * 2
     operands = (bins, row_proj, col_proj, conv_weight, conv_bias)
     out = pl.pallas_call(
         functools.partial(decoder, rows, cols),
@@ -337,8 +384,8 @@
             pltpu.VMEM((count, 2 * span, LANES), jnp.bfloat16),
             pltpu.VMEM((2, frame, LANES), jnp.float32),
             pltpu.VMEM((2, pitch + 2 * EDGE, LANES), jnp.float32),
-            pltpu.VMEM((2, frame * pitch + 2 * EDGE, LANES), jnp.float32),
-            pltpu.VMEM((2, frame // 2 * pitch, PAIR), jnp.bfloat16),
+            pltpu.VMEM((3, frame * pitch + 2 * EDGE, LANES), jnp.float32),
+            pltpu.VMEM((4 if 4 * stack <= SPARE else 2, frame // 2 * pitch, PAIR), jnp.bfloat16),
             pltpu.VMEM((5, 2 * PAIR, 2 * LANES), jnp.bfloat16),
             pltpu.VMEM((channels * tile_rows, tile_cols), jnp.float32),
             pltpu.SemaphoreType.DMA((5,)),

time: 25.5 us -> 21.6 us (0.85)
  Pallas kernels: 23.6 us -> 19.6 us
    pallas_call x1, Pallas kernels: 23.6 us -> 19.6 us  [shards(): pl.pallas_call(functools.partial(decoder, rows, cols), out_shape=jax.Shap...]
where the time goes in v3:
time: 21.6 us; the launch traced here: 21.4 us
  Pallas kernels  19.6 us (91%)
  local copies, waits for them, and re-layouts  1.77 us (8%)
    pallas_call x1, Pallas kernels, shards(): pl.pallas_call(functools.partial(decoder, rows, cols), out_shape=jax.Shap...  19.6 us
    unnamed x1, local copies, waits for them, and re-layouts  1.77 us

profile of v3, /device:TPU:0, one launch (start us, length us, event | category | flops | bytes accessed | tf_op | source)
XLA Modules:
  0.0 21.4 jit_solution(11188365359944120917)
XLA Ops:
  0.0 19.6 %decode_map.1 = bf16[96,16,128]{2,1,0:T(8,128)(2,1)} custom-call(bf16[8,1536]{1,0:T(8,128)(2,1)} %bins_hbm.1, bf16[96,1536]{1,0:T(8,128)(2,1)} %rp_hbm.1, bf16[96,1536]{1,0:T(8,128)(2,1)} %cp_hbm.1, bf16[3,9,96,96]{3,2,1,0:T(8,128)(2,1)} %w_hbm.1, f32[3,96]{1,0:T(4,128)} %b_hbm.1), custom_call_target="tpu_custom_call" | custom-call | tf_op jit(solution)/shard_map/decode_map/pallas_call | solution.py:377
  19.6 1.8 %copy.7 = bf16[96,16,128]{2,1,0:T(8,128)(2,1)} copy(bf16[96,16,128]{2,1,0:T(8,128)(2,1)} %decode_map.1) | data formatting | bytes 786432

commit v4 on v3

--- a/solution.py
+++ b/solution.py
@@ -13,7 +13,7 @@
 GROUP = 3 * LANES
 PAIR = 2 * GROUP
 NT = (((1,), (1,)), ((), ()))
-ROWS_PER_DOT = 512
+ROWS_PER_DOT = 1024
 MOST_CHUNKS = 16
 SPARE = 24 * 2**20
 

time: 21.6 us -> 21.6 us (level)
  no operation moved by 1% of the time
where the time goes in v4:
time: 21.6 us; the launch traced here: 21.5 us
  Pallas kernels  19.7 us (91%)
  local copies, waits for them, and re-layouts  1.77 us (8%)
    pallas_call x1, Pallas kernels, shards(): pl.pallas_call(functools.partial(decoder, rows, cols), out_shape=jax.Shap...  19.7 us
    unnamed x1, local copies, waits for them, and re-layouts  1.77 us

profile of v4, /device:TPU:0, one launch (start us, length us, event | category | flops | bytes accessed | tf_op | source)
XLA Modules:
  0.0 21.5 jit_solution(10517267613636662620)
XLA Ops:
  0.0 19.7 %decode_map.1 = bf16[96,16,128]{2,1,0:T(8,128)(2,1)} custom-call(bf16[8,1536]{1,0:T(8,128)(2,1)} %bins_hbm.1, bf16[96,1536]{1,0:T(8,128)(2,1)} %rp_hbm.1, bf16[96,1536]{1,0:T(8,128)(2,1)} %cp_hbm.1, bf16[3,9,96,96]{3,2,1,0:T(8,128)(2,1)} %w_hbm.1, f32[3,96]{1,0:T(4,128)} %b_hbm.1), custom_call_target="tpu_custom_call" | custom-call | tf_op jit(solution)/shard_map/decode_map/pallas_call | solution.py:377
  19.7 1.8 %copy.7 = bf16[96,16,128]{2,1,0:T(8,128)(2,1)} copy(bf16[96,16,128]{2,1,0:T(8,128)(2,1)} %decode_map.1) | data formatting | bytes 786432

commit v5 on v3

--- a/solution.py
+++ b/solution.py
@@ -132,18 +132,20 @@
 
     for load in loads[3:]:
         load.wait()
-    for layer in range(3):
-        for tap in range(9):
-            filters = w_ref[layer, tap].astype(jnp.float32).T.astype(jnp.bfloat16)
-            for swapped in range(2 if layer < 2 else 1):
-                first, second = (tap % 3, tap // 3) if swapped else (tap // 3, tap % 3)
-                for parity in range(2):
-                    at = (first + parity) * GROUP + second * LANES
-                    packed[
-                        2 * layer + swapped,
-                        at : at + channels,
-                        parity * LANES : parity * LANES + channels,
-                    ] = filters
+    def pack(layer, tap):
+        filters = w_ref[layer, tap].astype(jnp.float32).T.astype(jnp.bfloat16)
+        for swapped in range(2 if layer < 2 else 1):
+            first, second = (tap % 3, tap // 3) if swapped else (tap // 3, tap % 3)
+            for parity in range(2):
+                at = (first + parity) * GROUP + second * LANES
+                packed[
+                    2 * layer + swapped,
+                    at : at + channels,
+                    parity * LANES : parity * LANES + channels,
+                ] = filters
+
+    for tap in range(9):
+        pack(0, tap)
     fill = jnp.zeros((1, LANES - channels), jnp.float32)
     biases = [jnp.concatenate([b_ref[l : l + 1, :], fill], axis=1) for l in range(3)]
 
@@ -221,9 +223,13 @@
                         slice(parity * LANES, (parity + 1) * LANES),
                     )
 
-    def pipeline(groups, n, build, multiply, store):
+    def pipeline(groups, n, build, multiply, store, later):
         chunks = groups // n
+        pending = [(later, tap) for tap in range(9)] if later < 3 else []
+        quota = -(-len(pending) // chunks)
         if chunks > MOST_CHUNKS:
+            for item in pending:
+                pack(*item)
             lax.fori_loop(0, groups + 1, lambda i, c: (build(i), c)[1], 0)
             lax.fori_loop(0, chunks, lambda i, c: (store(i, multiply(i)), c)[1], 0)
             return
@@ -232,6 +238,8 @@
         held_acc = None
         for i in range(chunks):
             acc = multiply(i)
+            for item in pending[i * quota : (i + 1) * quota]:
+                pack(*item)
             if i + 1 < chunks:
                 for j in range(n):
                     build((i + 1) * n + 1 + j)
@@ -282,6 +290,7 @@
         build_first,
         lambda index: [convolved(side, side, index, n0, pitch) for side in range(2)],
         store_first,
+        1,
     )
 
     base1, spread1 = 4, 2
@@ -316,6 +325,7 @@
         build_second,
         lambda index: [convolved(apart + side, 2 + side, index, n1, chunk1) for side in range(2)],
         store_second,
+        2,
     )
 
     base2, spread2 = EDGE, 4
@@ -341,7 +351,7 @@
             value = state[2, begin, :] + acc[pixels, lanes] + biases[2]
             result[pl.ds(row, channels, stride=tile_rows), :] = value.T[:channels]
 
-    pipeline(groups2, n2, build_third, lambda index: convolved(0, 4, index, n2, chunk2), store_third)
+    pipeline(groups2, n2, build_third, lambda index: convolved(0, 4, index, n2, chunk2), store_third, 3)
     out_ref[...] = result[...].reshape(channels, tile_rows, tile_cols).astype(jnp.bfloat16)
 
     def sent(step, carry):
@@ -376,7 +386,7 @@
     operands = (bins, row_proj, col_proj, conv_weight, conv_bias)
     out = pl.pallas_call(
         functools.partial(decoder, rows, cols),
-        out_shape=jax.ShapeDtypeStruct((channels, tile_rows, tile_cols), jnp.bfloat16),
+        out_shape=pltpu.VMEM((channels, tile_rows, tile_cols), jnp.bfloat16),
         in_specs=[pl.BlockSpec(memory_space=pltpu.MemorySpace.HBM)] * 5,
         out_specs=pl.BlockSpec(memory_space=pltpu.VMEM),
         scratch_shapes=[pltpu.VMEM(x.shape, x.dtype) for x in operands]

time: 21.6 us -> 19.9 us (0.921)
  local copies, waits for them, and re-layouts: 1.77 us -> 0.75 us
  Pallas kernels: 19.6 us -> 19 us
    unnamed x1, local copies, waits for them, and re-layouts: 1.77 us -> 0.75 us
    pallas_call x1, Pallas kernels: 19.6 us -> 19 us  [shards(): pl.pallas_call(functools.partial(decoder, rows, cols), out_shape=pltpu.VM...]
where the time goes in v5:
time: 19.9 us; the launch traced here: 19.7 us
  Pallas kernels  19 us (95%)
  local copies, waits for them, and re-layouts  0.75 us (4%)
    pallas_call x1, Pallas kernels, shards(): pl.pallas_call(functools.partial(decoder, rows, cols), out_shape=pltpu.VM...  19 us
    unnamed x1, local copies, waits for them, and re-layouts  0.75 us

profile of v5, /device:TPU:0, one launch (start us, length us, event | category | flops | bytes accessed | tf_op | source)
XLA Modules:
  0.0 19.7 jit_solution(12906221750649189119)
XLA Ops:
  0.0 19.0 %decode_map.1 = bf16[96,16,128]{2,1,0:T(8,128)(2,1)S(1)} custom-call(bf16[8,1536]{1,0:T(8,128)(2,1)} %bins_hbm.1, bf16[96,1536]{1,0:T(8,128)(2,1)} %rp_hbm.1, bf16[96,1536]{1,0:T(8,128)(2,1)} %cp_hbm.1, bf16[3,9,96,96]{3,2,1,0:T(8,128)(2,1)} %w_hbm.1, f32[3,96]{1,0:T(4,128)} %b_hbm.1), custom_call_target="tpu_custom_call" | custom-call | tf_op jit(solution)/shard_map/decode_map/pallas_call | solution.py:387
  19.0 0.7 %copy.7 = bf16[96,16,128]{2,1,0:T(8,128)(2,1)} copy(bf16[96,16,128]{2,1,0:T(8,128)(2,1)S(1)} %decode_map.1) | data formatting | bytes 786432

commit v6 on v5

--- a/solution.py
+++ b/solution.py
@@ -71,32 +71,41 @@
     for load in loads:
         load.start()
 
-    def uses(block, other):
-        near_block = lax.div(other, cols) * (tile_rows // span)
-        far_block = lax.rem(other, cols) * (tile_cols // span)
+    def uses(row, col, block):
+        near_block = row * (tile_rows // span)
+        far_block = col * (tile_cols // span)
         return ((block >= near_block - 1) & (block <= near_block + tile_rows // span)) | (
             (block >= far_block - 1) & (block <= far_block + tile_cols // span)
         )
 
-    def ahead(step):
-        return lax.rem(me + step, count)
-
-    def behind(step):
-        return lax.rem(me + count - step, count)
-
-    def place(other):
-        return {"row": lax.div(other, cols), "col": lax.rem(other, cols)}
+    def around(visit, start):
+        def one(step, carry):
+            row = row_index + step
+            row = jnp.where(row >= rows, row - rows, row)
+            for col in range(cols):
+                carry = visit(row, col, row * cols + col, carry)
+            return carry
+
+        return lax.fori_loop(0, rows, one, start)
+
+    def sends_to(row, col, other):
+        return (other != me) & uses(row, col, me)
+
+    def comes_from(other):
+        return (other != me) & uses(row_index, col_index, other)
 
     barrier = pltpu.get_barrier_semaphore()
 
-    def greet(step, targets):
-        @pl.when(uses(behind(step), me))
+    def greet(row, col, other, targets):
+        @pl.when(comes_from(other))
         def _():
-            pl.semaphore_signal(barrier, inc=1, device_id=place(behind(step)), device_id_type=MESH)
-
-        return targets + jnp.where(uses(me, ahead(step)), 1, 0)
-
-    targets = lax.fori_loop(1, count, greet, 0)
+            pl.semaphore_signal(
+                barrier, inc=1, device_id={"row": row, "col": col}, device_id_type=MESH
+            )
+
+        return targets + jnp.where(sends_to(row, col, other), 1, 0)
+
+    targets = around(greet, 0)
     near_ref[...] = jnp.zeros_like(near_ref)
     far_ref[...] = jnp.zeros_like(far_ref)
     packed[...] = jnp.zeros_like(packed)
@@ -111,24 +120,24 @@
     held[me] = jnp.concatenate([jnp.concatenate(terms, axis=0), blank], axis=1).astype(jnp.bfloat16)
     pl.semaphore_wait(barrier, targets)
 
-    def copy(step):
+    def copy(row, col, target, source):
         return pltpu.make_async_remote_copy(
             src_ref=held.at[me],
             dst_ref=held.at[me],
-            send_sem=send_sem.at[step],
-            recv_sem=recv_sem.at[step],
-            device_id=place(ahead(step)),
+            send_sem=send_sem.at[target],
+            recv_sem=recv_sem.at[source],
+            device_id={"row": row, "col": col},
             device_id_type=MESH,
         )
 
-    def send(step, carry):
-        @pl.when(uses(me, ahead(step)))
+    def send(row, col, other, carry):
+        @pl.when(sends_to(row, col, other))
         def _():
-            copy(step).start()
+            copy(row, col, other, me).start()
 
         return carry
 
-    lax.fori_loop(1, count, send, 0)
+    around(send, 0)
 
     for load in loads[3:]:
         load.wait()
@@ -149,14 +158,14 @@
     fill = jnp.zeros((1, LANES - channels), jnp.float32)
     biases = [jnp.concatenate([b_ref[l : l + 1, :], fill], axis=1) for l in range(3)]
 
-    def finish(step, carry):
-        @pl.when(uses(behind(step), me))
+    def finish(row, col, other, carry):
+        @pl.when(comes_from(other))
         def _():
-            copy(step).wait_recv()
+            copy(row, col, other, other).wait_recv()
 
         return carry
 
-    lax.fori_loop(1, count, finish, 0)
+    around(finish, 0)
 
     def lay(out, first, blocks, offset):
         def one(index, carry):
@@ -354,14 +363,14 @@
     pipeline(groups2, n2, build_third, lambda index: convolved(0, 4, index, n2, chunk2), store_third, 3)
     out_ref[...] = result[...].reshape(channels, tile_rows, tile_cols).astype(jnp.bfloat16)
 
-    def sent(step, carry):
-        @pl.when(uses(me, ahead(step)))
+    def sent(row, col, other, carry):
+        @pl.when(sends_to(row, col, other))
         def _():
-            copy(step).wait_send()
+            copy(row, col, other, me).wait_send()
 
         return carry
 
-    lax.fori_loop(1, count, sent, 0)
+    around(sent, 0)
 
 
 def shards(bins, row_proj, col_proj, conv_weight, conv_bias):

time: 19.9 us -> 19.5 us (0.980)
  Pallas kernels: 19 us -> 18.6 us
    pallas_call x1, Pallas kernels: 19 us -> 18.6 us  [shards(): pl.pallas_call(functools.partial(decoder, rows, cols), out_shape=pltpu.VM...]
where the time goes in v6:
time: 19.5 us; the launch traced here: 19.4 us
  Pallas kernels  18.6 us (95%)
  local copies, waits for them, and re-layouts  0.75 us (4%)
    pallas_call x1, Pallas kernels, shards(): pl.pallas_call(functools.partial(decoder, rows, cols), out_shape=pltpu.VM...  18.6 us
    unnamed x1, local copies, waits for them, and re-layouts  0.75 us

profile of v6, /device:TPU:0, one launch (start us, length us, event | category | flops | bytes accessed | tf_op | source)
XLA Modules:
  0.0 19.4 jit_solution(17877490671575376491)
XLA Ops:
  0.0 18.6 %decode_map.1 = bf16[96,16,128]{2,1,0:T(8,128)(2,1)S(1)} custom-call(bf16[8,1536]{1,0:T(8,128)(2,1)} %bins_hbm.1, bf16[96,1536]{1,0:T(8,128)(2,1)} %rp_hbm.1, bf16[96,1536]{1,0:T(8,128)(2,1)} %cp_hbm.1, bf16[3,9,96,96]{3,2,1,0:T(8,128)(2,1)} %w_hbm.1, f32[3,96]{1,0:T(4,128)} %b_hbm.1), custom_call_target="tpu_custom_call" | custom-call | tf_op jit(solution)/shard_map/decode_map/pallas_call | solution.py:396
  18.6 0.7 %copy.7 = bf16[96,16,128]{2,1,0:T(8,128)(2,1)} copy(bf16[96,16,128]{2,1,0:T(8,128)(2,1)S(1)} %decode_map.1) | data formatting | bytes 786432

commit v7 on v6

--- a/solution.py
+++ b/solution.py
@@ -13,7 +13,7 @@
 GROUP = 3 * LANES
 PAIR = 2 * GROUP
 NT = (((1,), (1,)), ((), ()))
-ROWS_PER_DOT = 512
+ROWS_PER_DOT = 256
 MOST_CHUNKS = 16
 SPARE = 24 * 2**20
 

time: 19.5 us -> 19.4 us (level)
  no operation moved by 1% of the time
where the time goes in v7:
time: 19.4 us; the launch traced here: 19.3 us
  Pallas kernels  18.5 us (95%)
  local copies, waits for them, and re-layouts  0.75 us (4%)
    pallas_call x1, Pallas kernels, shards(): pl.pallas_call(functools.partial(decoder, rows, cols), out_shape=pltpu.VM...  18.5 us
    unnamed x1, local copies, waits for them, and re-layouts  0.75 us

profile of v7, /device:TPU:0, one launch (start us, length us, event | category | flops | bytes accessed | tf_op | source)
XLA Modules:
  0.0 19.3 jit_solution(13262155483533250687)
XLA Ops:
  0.0 18.5 %decode_map.1 = bf16[96,16,128]{2,1,0:T(8,128)(2,1)S(1)} custom-call(bf16[8,1536]{1,0:T(8,128)(2,1)} %bins_hbm.1, bf16[96,1536]{1,0:T(8,128)(2,1)} %rp_hbm.1, bf16[96,1536]{1,0:T(8,128)(2,1)} %cp_hbm.1, bf16[3,9,96,96]{3,2,1,0:T(8,128)(2,1)} %w_hbm.1, f32[3,96]{1,0:T(4,128)} %b_hbm.1), custom_call_target="tpu_custom_call" | custom-call | tf_op jit(solution)/shard_map/decode_map/pallas_call | solution.py:396
  18.5 0.7 %copy.7 = bf16[96,16,128]{2,1,0:T(8,128)(2,1)} copy(bf16[96,16,128]{2,1,0:T(8,128)(2,1)S(1)} %decode_map.1) | data formatting | bytes 786432
